TPU v7x, 256 devices: a whole 4x4x8 slice. The times are simulated.
256 devices in a mesh: front: 2 (over core), grid: 128 (over y, x, z).
Axes of the slice: x: 4, y: 4, z: 8, core: 2. Of those that a mesh axis runs over, the one named last changes fastest.
Arguments:
- child_schur: float32 [2, 2, 8192, 8192], P('front', None, 'grid'), as said below
- child_map: int32 [2, 2, 64], replicated, may hold values from 0 to 95, as said below
- orig_columns: float32 [2, 12288, 384], P('front', 'grid')
Outputs:
- factor_panel: float32 [2, 12288, 384], P('front', 'grid')
- schur_front: float32 [2, 12288, 12288], P('front', 'grid')
Inputs may be any that keep to these rules, and one draw needn't show every extreme that they name: Each row child_map[p, k, :] is strictly increasing and holds 0 and 95. `child_schur`: each child front is symmetric; the first 384 rows of each orig_columns[p] form a symmetric block, and each first 384 rows of panel_block are symmetric positive definite.
All inputs are finite; a program needn't handle non-finite values.
Results may differ from a plain program's by a relative error of at most 0.0001.
Values sent between devices are 32-bit elements; how exact they have to be, the bound alone decides.
A program may use at most 128 MiB of HBM per device.

v0:
```python
import jax
import jax.numpy as jnp
from jax import lax
from jax.sharding import PartitionSpec as P

P_SIZE = 12288
C = 8192
NB = 384
BLK = 128


def passed_along(array, axis, by):
    peers = lax.axis_size(axis)
    return lax.ppermute(array, axis, [(i, (i + by) % peers) for i in range(peers)])


def source_blocks(child_blocks):
    parent_ids = jnp.arange(P_SIZE // BLK, dtype=jnp.int32)
    matches = child_blocks[None, :] == parent_ids[:, None]
    present = jnp.any(matches, axis=1)
    child_ids = jnp.arange(child_blocks.shape[0], dtype=jnp.int32)
    anchor = jnp.sum(jnp.where(matches, child_ids[None, :], 0), axis=1)
    return (anchor, present)


def spread_columns(child_rows, anchor, present):
    count = child_rows.shape[0]
    picked = jnp.take(child_rows.reshape(count, C // BLK, BLK), anchor, axis=1)
    picked = jnp.where(present[None, :, None], picked, jnp.float32(0.0))
    return picked.reshape(count, P_SIZE)


def spread_rows(arrived, anchor, present):
    width = arrived.shape[1]
    picked = jnp.take(arrived.reshape(C // BLK, BLK, width), anchor, axis=0)
    picked = jnp.where(present[:, None, None], picked, jnp.float32(0.0))
    return picked.reshape(P_SIZE, width)


def on_device(child_schur, child_map, orig_columns):
    holder = lax.axis_index("front")
    front_count = lax.axis_size("front")

    def blocks_for(parent, child):
        return source_blocks(
            lax.dynamic_index_in_dim(child_map[:, child], parent, 0, keepdims=False)
        )

    own_anchor, own_present = blocks_for(holder, 0)
    near_anchor, near_present = blocks_for(holder, 1)
    own_rows = child_schur[0, 0]
    held_rows = child_schur[0, 1]
    far_anchor, far_present = blocks_for((holder + front_count - 1) % front_count, 1)
    second_sent = spread_columns(held_rows, far_anchor, far_present)
    first_sent = spread_columns(own_rows, own_anchor, own_present)
    first_got, second_got = (
        lax.all_to_all(first_sent, "grid", split_axis=1, concat_axis=0, tiled=True),
        lax.all_to_all(second_sent, "grid", split_axis=1, concat_axis=0, tiled=True),
    )
    second_got = passed_along(second_got, "front", -1)
    assembled = (
        spread_rows(first_got, own_anchor, own_present)
        + spread_rows(second_got, near_anchor, near_present)
    ).T
    local_rows = assembled.shape[0]
    start = lax.axis_index("grid") * local_rows
    row_ids = start + jnp.arange(local_rows, dtype=jnp.int32)
    column_ids = jnp.arange(P_SIZE, dtype=jnp.int32)
    panel_block = assembled[:, :NB] + orig_columns[0]
    padded = jnp.zeros((NB + local_rows, NB), jnp.float32)
    padded = lax.dynamic_update_slice(padded, panel_block, (jnp.minimum(start, NB), jnp.int32(0)))
    pivot_block = lax.psum(padded[:NB], "grid")
    pivot_factor = jnp.linalg.cholesky(pivot_block)
    solved = jax.scipy.linalg.solve_triangular(pivot_factor, panel_block.T, lower=True).T
    pivot_rows = jnp.take(pivot_factor, jnp.clip(row_ids, 0, NB - 1), axis=0)
    factor = jnp.where((row_ids < NB)[:, None], pivot_rows, solved)
    product = lax.dot_general(
        factor,
        lax.all_gather(factor, "grid", axis=0, tiled=True),
        (((1,), (1,)), ((), ())),
        precision=lax.Precision.HIGHEST,
    )
    inside = (row_ids >= NB)[:, None] & (column_ids >= NB)[None, :]
    schur_block = jnp.where(inside, assembled - product, jnp.float32(0.0))
    return (factor[None], schur_block[None])


def solution(mesh):
    placed = (P("front", None, "grid", None), P(), P("front", "grid", None))
    return jax.shard_map(
        on_device,
        mesh=mesh,
        in_specs=placed,
        out_specs=(P("front", "grid", None), P("front", "grid", None)),
        check_vma=False,
    )
```

profile of v0, /device:TPU:1, one launch (start us, length us, event | category | flops | bytes accessed | tf_op | source)
XLA Modules:
  0.0 786.0 jit_solution(10321800470050822554)
XLA Ops:
  8.4 3.9 slice_bitcast_fusion.1
  23.0 6.6 copy.78
  29.6 26.6 %all-to-all-start.1 = ((f32[64,128,96]{2,0,1:T(8,128)}), f32[64,128,96]{2,0,1:T(8,128)}, u32[]{:S(2)}, u32[]{:S(2)}) async-start(f32[64,128,96]{2,0,1:T(8,128)} %copy.78), calls=%async_computation.1 | async-start | bytes 8388608 | tf_op jit(solution)/shard_map/all_to_all | solution.py:58
  67.0 6.6 copy.74
  73.6 78.8 %all-to-all-done.1 = f32[64,128,96]{2,0,1:T(8,128)} async-done(((f32[64,128,96]{2,0,1:T(8,128)}), f32[64,128,96]{2,0,1:T(8,128)}, u32[]{:S(2)}, u32[]{:S(2)}) %all-to-all-start.1) | async-done | bytes 3145760 | tf_op jit(solution)/shard_map/all_to_all | solution.py:58
  152.5 7.4 all-to-all-start
  159.9 5.3 copy.79
  165.2 3.3 collective-permute-start
  168.7 85.4 %all-to-all-done = f32[64,128,96]{2,0,1:T(8,128)} async-done(((f32[64,128,96]{2,0,1:T(8,128)}), f32[64,128,96]{2,0,1:T(8,128)}, u32[]{:S(2)}, u32[]{:S(2)}) %all-to-all-start) | async-done | bytes 3145760 | tf_op jit(solution)/shard_map/all_to_all | solution.py:57
  254.1 4.0 copy.75
  263.4 3.0 gather_fusion.4
  266.4 5.8 fusion.2
  272.2 6.2 copy.81
  282.4 210.4 %all-reduce.3.cloned.1.call-done = f32[384,384]{0,1:T(8,128)} async-done(((f32[384,384]{0,1:T(8,128)}), f32[384,384]{0,1:T(8,128)}) %all-reduce.3.cloned.1.call-update) | async-done | bytes 589840 | tf_op jit(solution)/shard_map/psum | solution.py:72
  495.2 11.7 %cholesky.77 = f32[128,128]{1,0:T(8,128)S(1)} custom-call(f32[128,128]{1,0:T(8,128)S(1)} %cholesky.192), custom_call_target="Cholesky" | custom-call | tf_op jit(solution)/shard_map/jit(cholesky)/cholesky | solution.py:73
  507.6 9.8 %custom-call.23 = f32[1,128,128]{1,2,0:T(8,128)S(1)} custom-call(f32[1,128,128]{2,1,0:T(8,128)S(1)} %get-tuple-element.46), custom_call_target="InvertDiagBlocksLowerTriangular" | custom-call | tf_op jit(solution)/shard_map/jit(cholesky)/cholesky | solution.py:73
  518.0 11.7 %cholesky.162 = f32[128,128]{1,0:T(8,128)S(1)} custom-call(f32[128,128]{1,0:T(8,128)S(1)} %cholesky.196), custom_call_target="Cholesky" | custom-call | tf_op jit(solution)/shard_map/jit(cholesky)/cholesky | solution.py:73
  530.5 10.0 %custom-call.24 = f32[1,128,128]{1,2,0:T(8,128)S(1)} custom-call(f32[1,128,128]{2,1,0:T(8,128)S(1)} %get-tuple-element.43), custom_call_target="InvertDiagBlocksLowerTriangular" | custom-call | tf_op jit(solution)/shard_map/jit(cholesky)/cholesky | solution.py:73
  540.9 11.7 %cholesky.181 = f32[128,128]{1,0:T(8,128)S(1)} custom-call(f32[128,128]{1,0:T(8,128)S(1)} %convolution_subtract_fusion.4), custom_call_target="Cholesky" | custom-call | tf_op jit(solution)/shard_map/jit(cholesky)/cholesky | solution.py:73
  555.3 6.4 while.1
  561.7 29.5 %custom-call.25 = f32[3,128,128]{1,2,0:T(8,128)S(1)} custom-call(f32[3,128,128]{2,1,0:T(8,128)S(1)} %get-tuple-element.11), custom_call_target="InvertDiagBlocksLowerTriangular" | custom-call | tf_op jit(solution)/shard_map/jit(_solve_triangular)/triangular_solve | solution.py:74
  594.0 158.6 %all-gather.2.cloned.1.call-done = f32[12288,384]{1,0:T(8,128)} async-done(((f32[96,384]{1,0:T(8,128)}), f32[12288,384]{1,0:T(8,128)}) %all-gather.2.cloned.1.call-update) | async-done | bytes 18874384 | tf_op jit(solution)/shard_map/all_gather | solution.py:79
  752.6 20.3 %fusion.1 = f32[1,96,12288]{1,2,0:T(8,128)} fusion(f32[96,12288]{0,1:T(8,128)} %bitcast.88, f32[96,384]{1,0:T(8,128)} %fusion.5, f32[12288,384]{1,0:T(8,128)} %all-gather.2.cloned.1.call-done, pred[96]{0:T(512)(128)(4,1)S(1)} %fusion.29, pred[12288]{0:T(1024)(128)(4,1)S(1)} %iota_compare_fusion.3), kind=kOutput, calls=%fused_computation.9 | convolution fusion | flops 5439356928 | bytes 28471392 | tf_op jit(solution)/shard_map/dot_general | solution.py:77
  772.9 6.1 copy.87
  (83 shorter events, 46.8 us)
Async XLA Ops:
  29.6 26.6 %copy-start = (f32[8,8,64,128]{3,1,2,0:T(8,128)S(1)}, f32[8,8,64,128]{3,1,2,0:T(8,128)}, u32[]{:S(2)}) copy-start(f32[8,8,64,128]{3,1,2,0:T(8,128)} %get-tuple-element.38) | copy-start | bytes 6291460
  29.6 122.9 %all-to-all-start.1 = ((f32[64,128,96]{2,0,1:T(8,128)}), f32[64,128,96]{2,0,1:T(8,128)}, u32[]{:S(2)}, u32[]{:S(2)}) async-start(f32[64,128,96]{2,0,1:T(8,128)} %copy.78), calls=%async_computation.1 | async-start | bytes 8388608 | tf_op jit(solution)/shard_map/all_to_all | solution.py:58
  152.5 101.7 %all-to-all-start = ((f32[64,128,96]{2,0,1:T(8,128)}), f32[64,128,96]{2,0,1:T(8,128)}, u32[]{:S(2)}, u32[]{:S(2)}) async-start(f32[64,128,96]{2,0,1:T(8,128)} %copy.74), calls=%async_computation | async-start | bytes 8388608 | tf_op jit(solution)/shard_map/all_to_all | solution.py:57
  159.8 332.9 %all-reduce.3.cloned.1.call-start = ((), (), s32[]{:S(2)}) async-start(), calls=%async_computation.2 | async-start | bytes 1179648 | tf_op jit(solution)/shard_map/psum | solution.py:72
  159.9 8.6 %copy-start.1 = (f32[1,96,384]{2,1,0:T(8,128)S(1)}, f32[1,96,384]{2,1,0:T(8,128)}, u32[]{:S(2)}) copy-start(f32[1,96,384]{2,1,0:T(8,128)} %param.9) | copy-start | bytes 442372
  165.2 95.9 %collective-permute-start = (f32[8192,96]{0,1:T(8,128)}, f32[8192,96]{0,1:T(8,128)}, u32[]{:S(2)}, u32[]{:S(2)}) collective-permute-start(f32[8192,96]{0,1:T(8,128)} %copy.79), channel_id=1, source_target_pairs={{0,128},{128,0},{1,129},{129,1},{2,130},{130,2},{3,131},{131,3},{4... | collective-permute-start | bytes 9437192 | tf_op jit(solution)/shard_map/ppermute | solution.py:14
  281.9 470.8 %all-gather.2.cloned.1.call-start = ((), (), s32[]{:S(2)}) async-start(), calls=%async_computation.3 | async-start | bytes 19021824 | tf_op jit(solution)/shard_map/all_gather | solution.py:79
Sparse Core Ops, SparseCore 0:
  282.0 210.7 all-reduce.2
  594.1 158.4 all-gather.1
where the time goes:
time: 794 us; the launch traced here: 786 us
  waiting for transfers between devices  533 us (67%)
  other arithmetic  100 us (13%)
  local copies, waits for them, and re-layouts  75.6 us (10%)
  starting transfers between devices  37.8 us (5%)
  matrix products  22.6 us (3%)
  between operations  16.5 us (2%)
    psum x1, waiting for transfers between devices, on_device(): pivot_block = lax.psum(padded[:NB], 'grid')  210 us
    all_gather x1, waiting for transfers between devices, on_device(): lax.all_gather(factor, 'grid', axis=0, tiled=True)  159 us
    all_to_all x1, waiting for transfers between devices, on_device(): lax.all_to_all(first_sent, 'grid', split_axis=1, concat_axis=0, tiled=True)  85.4 us
    all_to_all x1, waiting for transfers between devices, on_device(): lax.all_to_all(second_sent, 'grid', split_axis=1, concat_axis=0, tiled=True)  78.8 us
    another operation x11, other arithmetic, on_device(): pivot_factor = jnp.linalg.cholesky(pivot_block)  57 us
    another operation x3, other arithmetic, on_device(): jax.scipy.linalg.solve_triangular(pivot_factor, panel_block.T, lower=True)  29.6 us
    all_to_all x1, starting transfers between devices, on_device(): lax.all_to_all(second_sent, 'grid', split_axis=1, concat_axis=0, tiled=True)  26.6 us
    dot_general x1, matrix products, on_device(): lax.dot_general(factor, lax.all_gather(factor, 'grid', axis=0, tiled=True...  20.3 us
  transfers between devices with their start and end apart: 5, of which 4 were waited for; matrix products, arithmetic and copies ran while one was open for 3% of the time, Pallas kernels for 0%

commit v1 on v0

v1 whole, which is shorter than its diff:
```python
import functools

import jax
import jax.numpy as jnp
from jax import lax
from jax.experimental import pallas as pl
from jax.experimental.pallas import tpu as pltpu
from jax.sharding import PartitionSpec as P

NB = 384
BLK = 128
PROWS = 96
CROWS = 64
GRID_SHAPE = (4, 4, 8)
MESH = pl.DeviceIdType.MESH
HIGHEST = lax.Precision.HIGHEST


def scan_sources(map_ref, parent, anchor, present, blocks):
    for child in range(2):
        def step(block, at, child=child):
            found = (map_ref[parent, child, at] == block).astype(jnp.int32)
            anchor[child, block] = at
            present[child, block] = found
            return at + found
        lax.fori_loop(0, blocks, lambda b, at: jnp.minimum(step(b, at), map_ref.shape[2] - 1), jnp.int32(0))


def joined(even, odd, child):
    lanes = lax.broadcasted_iota(jnp.int32, even.shape, 1)
    if child == 0:
        return jnp.where(lanes < CROWS, even, pltpu.roll(odd, CROWS, 1))
    return jnp.where(lanes < CROWS, pltpu.roll(even, CROWS, 1), odd)


def comm_kernel(
    shape, map_ref, schur, orig, got, panels,
    anchor, present, first, second, tiles, spread, after_z, after_x, corner, orig_v, panel_v,
    swap_sem, load_sem, z_send, z_recv, z_own, x_send, x_recv, x_own, y_send, y_recv,
    p_send, p_recv, p_own,
):
    ny, nx, nz = shape
    count = ny * nx * nz
    front = lax.axis_index("front")
    grid = lax.axis_index("grid")
    y = grid // (nx * nz)
    x = lax.rem(grid // nz, nx)
    z = lax.rem(grid, nz)

    def at(yy, xx, zz):
        return (front, (yy * nx + xx) * nz + zz)

    barrier = pltpu.get_barrier_semaphore()
    other = (1 - front, grid)
    pl.semaphore_signal(barrier, inc=1, device_id=other, device_id_type=MESH)
    for by in range(1, nz):
        pl.semaphore_signal(barrier, inc=1, device_id=at(y, x, lax.rem(z + by, nz)), device_id_type=MESH)
    for by in range(1, nx):
        pl.semaphore_signal(barrier, inc=1, device_id=at(y, lax.rem(x + by, nx), z), device_id_type=MESH)
    for by in range(1, ny):
        pl.semaphore_signal(barrier, inc=1, device_id=at(lax.rem(y + by, ny), x, z), device_id_type=MESH)
    load = pltpu.make_async_copy(schur.at[0], first, load_sem.at[0])
    load.start()
    load_orig = pltpu.make_async_copy(orig, orig_v, load_sem.at[1])
    load_orig.start()
    pl.semaphore_wait(barrier, 1 + (nz - 1) + (nx - 1) + (ny - 1))
    swap = pltpu.make_async_remote_copy(
        src_ref=schur.at[1], dst_ref=second, send_sem=swap_sem.at[0], recv_sem=swap_sem.at[1],
        device_id=other, device_id_type=MESH,
    )
    swap.start()
    scan_sources(map_ref, front, anchor, present, count * PROWS // BLK)
    load.wait()
    swap.wait()
    for child, held in ((0, first), (1, second)):
        for i in range(tiles.shape[1]):
            tiles[child, i] = held[:, i * BLK:(i + 1) * BLK]

    chunks = list(range(ny // 2, 0, -1)) + list(range(ny // 2 + 1, ny)) + [0]
    offsets = sorted(range(1, nz), key=lambda by: -min(by, nz - by))
    groups = nx * nz // 4
    z_copies, x_copies, y_copies = {}, {}, []

    for c in chunks:
        yc = lax.rem(y + c, ny)

        def build(h, carry, yc=yc):
            for i in range(3):
                block = yc * (3 * groups) + 3 * h + i
                parts = []
                for child in range(2):
                    tile = tiles[child, anchor[child, block]]
                    parts.append(tile * present[child, block].astype(jnp.float32))
                turned = jnp.concatenate(parts, axis=0).T
                for q in range(4):
                    unit = 4 * i + q
                    device = 4 * h + unit // 3
                    spread[yc, device // nz, lax.rem(device, nz), unit % 3] = turned[32 * q:32 * q + 32]
            return carry

        lax.fori_loop(0, groups, build, 0)
        for n, by in enumerate(offsets):
            to = lax.rem(z + by, nz)
            copy = pltpu.make_async_remote_copy(
                src_ref=spread.at[yc, :, to], dst_ref=after_z.at[z, yc],
                send_sem=z_send.at[c, n], recv_sem=z_recv.at[c, n],
                device_id=at(y, x, to), device_id_type=MESH,
            )
            copy.start()
            z_copies[c, n] = copy
        own = pltpu.make_async_copy(spread.at[yc, :, z], after_z.at[z, yc], z_own.at[c])
        own.start()
        z_copies[c, "own"] = own

    def start_x(c):
        yc = lax.rem(y + c, ny)
        for n in range(len(offsets)):
            z_copies[c, n].wait_recv()
        z_copies[c, "own"].wait()
        land = got if c == 0 else after_x
        for by in range(1, nx):
            to = lax.rem(x + by, nx)
            copy = pltpu.make_async_remote_copy(
                src_ref=after_z.at[:, yc, to], dst_ref=land.at[yc, x],
                send_sem=x_send.at[c, by], recv_sem=x_recv.at[c, by],
                device_id=at(y, to, z), device_id_type=MESH,
            )
            copy.start()
            x_copies[c, by] = copy
        own = pltpu.make_async_copy(after_z.at[:, yc, x], land.at[yc, x], x_own.at[c])
        own.start()
        x_copies[c, "own"] = own

    def finish_x(c):
        for by in range(1, nx):
            x_copies[c, by].wait_recv()
        x_copies[c, "own"].wait()

    def start_y(c):
        finish_x(c)
        yc = lax.rem(y + c, ny)
        copy = pltpu.make_async_remote_copy(
            src_ref=after_x.at[yc], dst_ref=got.at[y],
            send_sem=y_send.at[c], recv_sem=y_recv.at[c],
            device_id=at(yc, x, z), device_id_type=MESH,
        )
        copy.start()
        y_copies.append(copy)

    for n, c in enumerate(chunks):
        start_x(c)
        if n > 0:
            start_y(chunks[n - 1])
    finish_x(0)
    for copy in y_copies:
        copy.wait_recv()

    loads = []
    for d in range(6):
        copy = pltpu.make_async_copy(
            got.at[d // (nx * nz), (d // nz) % nx, d % nz], corner.at[d], load_sem.at[2 + d]
        )
        copy.start()
        loads.append(copy)
    load_orig.wait()
    for copy in loads:
        copy.wait()
    for block in range(3):
        value = orig_v[:, BLK * block:BLK * (block + 1)]
        for child in range(2):
            a = anchor[child, block]
            pair = [corner[2 * a + i].reshape(PROWS, BLK) for i in range(2)]
            value = value + present[child, block].astype(jnp.float32) * joined(pair[0], pair[1], child)
        panel_v[block] = value

    own = pltpu.make_async_copy(panel_v, panels.at[:, y, x, z], p_own)
    own.start()

    axes = {"y": (ny, y), "x": (nx, x), "z": (nz, z)}

    def neighbour(axis, by):
        size, here = axes[axis]
        there = lax.rem(here + by + size, size)
        return at(*[there if axis == a else axes[a][1] for a in "yxz"])

    def steps(part, order):
        whole = []
        for axis in order:
            size, here = axes[axis]
            index = [slice(None) if a in whole else axes[a][1] for a in "yxz"]
            for s in range(size // 2):
                half = s == size // 2 - 1
                yield axis, s, half, index, len(whole)
            whole.append(axis)

    def block_ref(part, axis, index, i, half):
        full = [i if a == axis else index[n] for n, a in enumerate("yxz")]
        rows = slice(None) if half is None else pl.ds(half * (PROWS // 2), PROWS // 2)
        return panels.at[(part, *full, rows)]

    own.wait()
    orders = ("zxy", "xyz", "yzx")
    plans = [list(steps(part, order)) for part, order in enumerate(orders)]
    pending = [[], [], []]
    sent = []
    for turn in range(max(len(p) for p in plans)):
        for part in range(3):
            if turn >= len(plans[part]):
                continue
            axis, s, half, index, _ = plans[part][turn]
            for copy in pending[part]:
                copy.wait_recv()
            pending[part] = []
            size, here = axes[axis]
            for way, by in ((0, 1), (1, -1)):
                origin = lax.rem(here - by * s + size, size)
                block = block_ref(part, axis, index, origin, way if half else None)
                copy = pltpu.make_async_remote_copy(
                    src_ref=block, dst_ref=block,
                    send_sem=p_send.at[part, turn, way], recv_sem=p_recv.at[part, turn, way],
                    device_id=neighbour(axis, by), device_id_type=MESH,
                )
                copy.start()
                pending[part].append(copy)
                sent.append(copy)
    for part in range(3):
        for copy in pending[part]:
            copy.wait_recv()
    swap_done = list(z_copies.items())
    for key, copy in swap_done:
        if key[1] != "own":
            copy.wait_send()
    for key, copy in x_copies.items():
        if key[1] != "own":
            copy.wait_send()
    for copy in y_copies:
        copy.wait_send()
    for copy in sent:
        copy.wait_send()


def exchange(shape, child_map, schur, orig):
    ny, nx, nz = shape
    count = ny * nx * nz
    blocks = count * PROWS // BLK
    unit = (3, 32, BLK)
    turns = (ny + nx + nz) // 2
    dma = pltpu.SemaphoreType.DMA
    hbm = pl.BlockSpec(memory_space=pl.ANY)
    return pl.pallas_call(
        functools.partial(comm_kernel, shape),
        out_shape=(
            jax.ShapeDtypeStruct((ny, nx, nz) + unit, jnp.float32),
            jax.ShapeDtypeStruct((3, ny, nx, nz, PROWS, BLK), jnp.float32),
        ),
        in_specs=[pl.BlockSpec(memory_space=pltpu.SMEM), hbm, hbm],
        out_specs=(hbm, hbm),
        scratch_shapes=[
            pltpu.SMEM((2, blocks), jnp.int32),
            pltpu.SMEM((2, blocks), jnp.int32),
            pltpu.VMEM(schur.shape[1:], jnp.float32),
            pltpu.VMEM(schur.shape[1:], jnp.float32),
            pltpu.VMEM((2, schur.shape[2] // BLK, CROWS, BLK), jnp.float32),
            pltpu.VMEM((ny, nx, nz) + unit, jnp.float32),
            pltpu.VMEM((nz, ny, nx) + unit, jnp.float32),
            pltpu.VMEM((ny, nx, nz) + unit, jnp.float32),
            pltpu.VMEM((6,) + unit, jnp.float32),
            pltpu.VMEM((PROWS, NB), jnp.float32),
            pltpu.VMEM((3, PROWS, BLK), jnp.float32),
            dma((2,)), dma((8,)),
            dma((ny, nz)), dma((ny, nz)), dma((ny,)),
            dma((ny, nx)), dma((ny, nx)), dma((ny,)),
            dma((ny,)), dma((ny,)),
            dma((3, turns, 2)), dma((3, turns, 2)), dma,
        ],
        compiler_params=pltpu.CompilerParams(
            collective_id=0, has_side_effects=True, vmem_limit_bytes=48 * 1024 * 1024
        ),
    )(child_map, schur, orig)


def update_kernel(shape, map_ref, front_ref, got, panels, weight, out, anchor, present):
    ny, nx, nz = shape
    count = ny * nx * nz
    step = pl.program_id(0)
    wide = nz * PROWS

    @pl.when(step == 0)
    def _():
        scan_sources(map_ref, front_ref[0], anchor, present, count * PROWS // BLK)

    product = jnp.zeros((PROWS, wide), jnp.float32)
    for part in range(3):
        columns = panels[part, 0, 0].reshape(wide, BLK)
        product += lax.dot_general(
            weight[:, part * BLK:(part + 1) * BLK], columns, (((1,), (1,)), ((), ())),
            precision=HIGHEST, preferred_element_type=jnp.float32,
        )
    rows = front_ref[1] * PROWS + lax.broadcasted_iota(jnp.int32, (PROWS, BLK), 0)
    for i in range(wide // BLK):
        block = step * (wide // BLK) + i
        value = -product[:, i * BLK:(i + 1) * BLK]
        for child in range(2):
            a = anchor[child, block]
            pair = [got[2 * a + n].reshape(PROWS, BLK) for n in range(2)]
            value = value + present[child, block].astype(jnp.float32) * joined(pair[0], pair[1], child)
        inside = (rows >= NB) & (block >= NB // BLK)
        out[:, i * BLK:(i + 1) * BLK] = jnp.where(inside, value, 0.0)


def update(shape, child_map, where, got, panels, weight):
    ny, nx, nz = shape
    count = ny * nx * nz
    blocks = count * PROWS // BLK
    wide = nz * PROWS
    smem = pl.BlockSpec(memory_space=pltpu.SMEM)
    return pl.pallas_call(
        functools.partial(update_kernel, shape),
        grid=(ny * nx,),
        out_shape=jax.ShapeDtypeStruct((PROWS, count * PROWS), jnp.float32),
        in_specs=[
            smem, smem,
            pl.BlockSpec((count, 3, 32, BLK), lambda i: (0, 0, 0, 0)),
            pl.BlockSpec((3, 1, 1, nz, PROWS, BLK), lambda i: (0, i // nx, i % nx, 0, 0, 0)),
            pl.BlockSpec((PROWS, NB), lambda i: (0, 0)),
        ],
        out_specs=pl.BlockSpec((PROWS, wide), lambda i: (0, i)),
        scratch_shapes=[pltpu.SMEM((2, blocks), jnp.int32), pltpu.SMEM((2, blocks), jnp.int32)],
        compiler_params=pltpu.CompilerParams(vmem_limit_bytes=48 * 1024 * 1024),
    )(child_map, where, got.reshape(count, 3, 32, BLK), panels, weight)


def on_device(shape, child_schur, child_map, orig_columns):
    got, panels = exchange(shape, child_map, child_schur[0], orig_columns[0])
    count = shape[0] * shape[1] * shape[2]
    grid = lax.axis_index("grid")
    by_row = panels.reshape(3, count, PROWS, BLK)
    pivot_block = by_row[:, :NB // PROWS].reshape(3, NB, BLK).transpose(1, 0, 2).reshape(NB, NB)
    own_panel = lax.dynamic_index_in_dim(by_row, grid, 1, keepdims=False).transpose(1, 0, 2).reshape(PROWS, NB)
    pivot_factor = jnp.linalg.cholesky(pivot_block)
    inverse = jax.scipy.linalg.solve_triangular(pivot_factor, jnp.eye(NB, dtype=jnp.float32), lower=True)
    solved = jnp.dot(own_panel, inverse.T, precision=HIGHEST)
    row_ids = grid * PROWS + jnp.arange(PROWS, dtype=jnp.int32)
    pivot_rows = jnp.take(pivot_factor, jnp.clip(row_ids, 0, NB - 1), axis=0)
    factor = jnp.where((row_ids < NB)[:, None], pivot_rows, solved)
    weight = jnp.dot(solved, inverse, precision=HIGHEST)
    where = jnp.stack([lax.axis_index("front"), grid]).astype(jnp.int32)
    schur_block = update(shape, child_map, where, got, panels, weight)
    return (factor[None], schur_block[None])


def solution(mesh):
    placed = (P("front", None, "grid", None), P(), P("front", "grid", None))
    count = mesh.shape["grid"]
    shape = GRID_SHAPE if count == 128 else (count // 8, 2, 4)
    return jax.shard_map(
        functools.partial(on_device, shape),
        mesh=mesh,
        in_specs=placed,
        out_specs=(P("front", "grid", None), P("front", "grid", None)),
        check_vma=False,
    )
```

time: 794 us -> 437 us (0.55)
  waiting for transfers between devices: 533 us -> 0 us
  Pallas kernels: 0 us -> 323 us
  local copies, waits for them, and re-layouts: 75.6 us -> 12 us
  starting transfers between devices: 37.8 us -> 0 us
  matrix products: 22.6 us -> 4.9 us
  between operations: 16.5 us -> 2.82 us
  other arithmetic: 100 us -> 86.8 us
    pallas_call x0 -> x2, Pallas kernels: none -> 323 us  [the longest x1 296 us: exchange(): pl.pallas_call(functools.partial(comm_kernel, shape), out_shape=(jax.Shap...]
    psum x1 -> x0, waiting for transfers between devices: 210 us -> none  [on_device(): pivot_block = lax.psum(padded[:NB], 'grid')]
    all_to_all x2 -> x0, waiting for transfers between devices: 164 us -> none  [the longest x1 85.4 us: on_device(): lax.all_to_all(first_sent, 'grid', split_axis=1, concat_axis=0, tiled=True)]
    all_gather x1 -> x0, waiting for transfers between devices: 159 us -> none  [on_device(): lax.all_gather(factor, 'grid', axis=0, tiled=True)]
    all_to_all x2 -> x0, starting transfers between devices: 34 us -> none  [the longest x1 26.6 us: on_device(): lax.all_to_all(second_sent, 'grid', split_axis=1, concat_axis=0, tiled=True)]
    all_to_all x5 -> x0, local copies, waits for them, and re-layouts: 23.6 us -> none  [the longest x3 14.5 us: on_device(): lax.all_to_all(second_sent, 'grid', split_axis=1, concat_axis=0, tiled=True)]
    dot_general x1 -> x2, matrix products: 20.3 us -> 2.14 us  [the longest x1 1.64 us: on_device(): solved = jnp.dot(own_panel, inverse.T, precision=HIGHEST)]
    gather x4 -> x0, local copies, waits for them, and re-layouts: 10.8 us -> none  [the longest x2 6.02 us: spread_rows(): picked = jnp.take(arrived.reshape(C // BLK, BLK, width), anchor, axis=0)]
  transfers between devices with their start and end apart: 5 -> 0, of which waited for: 4 -> 0; matrix products, arithmetic and copies ran while one was open for 3% -> 0% of each run, Pallas kernels for 0% -> 0%
where the time goes in v1:
time: 437 us; the launch traced here: 430 us
  Pallas kernels  323 us (74%)
  other arithmetic  86.8 us (20%)
  local copies, waits for them, and re-layouts  12 us (3%)
  matrix products  4.9 us (1%)
    pallas_call x1, Pallas kernels, exchange(): pl.pallas_call(functools.partial(comm_kernel, shape), out_shape=(jax.Shap...  296 us
    another operation x10, other arithmetic, on_device(): pivot_factor = jnp.linalg.cholesky(pivot_block)  56.2 us
    another operation x3, other arithmetic, on_device(): jax.scipy.linalg.solve_triangular(pivot_factor, jnp.eye(NB, dtype=jnp.flo...  29.6 us
    pallas_call x1, Pallas kernels, update(): pl.pallas_call(functools.partial(update_kernel, shape), grid=(ny * nx,),...  27.4 us

profile of v1, /device:TPU:1, one launch (start us, length us, event | category | flops | bytes accessed | tf_op | source)
XLA Modules:
  0.0 429.7 jit_solution(5345032765558035591)
XLA Ops:
  0.7 2.2 copy-done
  2.9 0.9 copy-done.1
  3.8 0.7 copy-done.2
  4.5 295.8 %shard_map.50 = (f32[4,4,8,3,32,128]{5,4,3,2,1,0:T(8,128)}, f32[3,4,4,8,96,128]{5,4,3,2,1,0:T(8,128)}) custom-call(s32[2,2,64]{2,1,0:T(2,128)S(1)} %copy-done.2, f32[2,64,8192]{2,1,0:T(8,128)S(1)} %bitcast.66, f32[96,384]{1,0:T(8,128)S(1)} %bitcast.67), custom_call_target="tpu_custom_call" | custom-call | tf_op jit(solution)/shard_map/pallas_call | solution.py:250
  300.3 1.1 slice.98
  301.9 11.7 %cholesky.77 = f32[128,128]{1,0:T(8,128)S(1)} custom-call(f32[128,128]{1,0:T(8,128)S(1)} %cholesky.192), custom_call_target="Cholesky" | custom-call | tf_op jit(solution)/shard_map/jit(cholesky)/cholesky | solution.py:340
  313.7 9.8 %custom-call.23 = f32[1,128,128]{1,2,0:T(8,128)S(1)} custom-call(f32[1,128,128]{2,1,0:T(8,128)S(1)} %get-tuple-element.32), custom_call_target="InvertDiagBlocksLowerTriangular" | custom-call | tf_op jit(solution)/shard_map/jit(cholesky)/cholesky | solution.py:340
  324.1 11.7 %cholesky.162 = f32[128,128]{1,0:T(8,128)S(1)} custom-call(f32[128,128]{1,0:T(8,128)S(1)} %cholesky.196), custom_call_target="Cholesky" | custom-call | tf_op jit(solution)/shard_map/jit(cholesky)/cholesky | solution.py:340
  335.9 9.9 %custom-call.24 = f32[1,128,128]{1,2,0:T(8,128)S(1)} custom-call(f32[1,128,128]{2,1,0:T(8,128)S(1)} %get-tuple-element.29), custom_call_target="InvertDiagBlocksLowerTriangular" | custom-call | tf_op jit(solution)/shard_map/jit(cholesky)/cholesky | solution.py:340
  346.2 11.7 %cholesky.181 = f32[128,128]{1,0:T(8,128)S(1)} custom-call(f32[128,128]{1,0:T(8,128)S(1)} %convolution_subtract_fusion.3), custom_call_target="Cholesky" | custom-call | tf_op jit(solution)/shard_map/jit(cholesky)/cholesky | solution.py:340
  358.0 0.7 compare_reduce_fusion.1
  359.9 0.6 compare_reduce_fusion
  361.3 5.9 %while.1 = (s32[]{:T(128)}, f32[384,384]{1,0:T(8,128)S(1)}, s32[3,2]{0,1:T(2,128)S(1)}, f32[3,128,128]{2,1,0:T(8,128)S(1)}, s32[]{:T(128)}) while((s32[]{:T(128)}, f32[384,384]{1,0:T(8,128)S(1)}, s32[3,2]{0,1:T(2,128)S(1)}, f32[3,128,128]{2,1,0:T(8,128)S(1)}, s32[]{:T(128)}) %tuple.31), condition=%wide.while_cond, body=%wide.while_body.sunk | while | flops 2 | bytes 131189 | solution.py:341
  361.4 0.5 fusion.35
  361.9 1.4 bitcast_dynamic-update-slice_fusion.2
  363.4 0.5 fusion.35
  363.9 1.4 bitcast_dynamic-update-slice_fusion.2
  365.4 0.5 fusion.35
  365.9 1.4 bitcast_dynamic-update-slice_fusion.2
  367.3 29.5 %custom-call.25 = f32[3,128,128]{1,2,0:T(8,128)S(1)} custom-call(f32[3,128,128]{2,1,0:T(8,128)S(1)} %get-tuple-element.13), custom_call_target="InvertDiagBlocksLowerTriangular" | custom-call | tf_op jit(solution)/shard_map/jit(_solve_triangular)/triangular_solve | solution.py:341
  398.6 1.6 fusion.3
  400.3 0.7 gather_fusion
  401.0 0.8 select_bitcast_fusion
  402.3 27.4 %shard_map.51 = f32[96,12288]{1,0:T(8,128)} custom-call(s32[2,2,64]{2,1,0:T(2,128)S(1)} %copy-done.3, s32[2]{0:T(128)S(1)} %pad_add_fusion.front_ref, f32[128,3,32,128]{3,2,1,0:T(8,128)} %bitcast.70, f32[3,4,4,8,96,128]{5,4,3,2,1,0:T(8,128)} %get-tuple-element.4.panels, f32[96,384]{1,0:T(8,128)S(1)} %fusion.2.weight), custom_call_target="tpu_custom_call" | custom-call | tf_op jit(solution)/shard_map/pallas_call | solution.py:317
  (37 shorter events, 4.5 us)
Async XLA Ops:
  0.6 401.7 %copy-start.3 = (s32[2,2,64]{2,1,0:T(2,128)S(1)}, s32[2,2,64]{2,1,0:T(2,128)}, u32[]{:S(2)}) copy-start(s32[2,2,64]{2,1,0:T(2,128)} %map_ref.3) | copy-start | bytes 3076
  0.7 2.2 copy-start
  2.9 0.9 copy-start.1
  3.8 0.7 copy-start.2
